TPU v7x, 512 devices: a whole 4x8x8 slice. The times are simulated.
512 devices in a mesh: ctx: 64 (over y_hi, z, core), tsp: 8 (over x, y_lo).
Axes of the slice: x: 4, y: 8 (y_hi: 4, y_lo: 2; y = y_hi * 2 + y_lo), z: 8, core: 2. Of those that a mesh axis runs over, the one named last changes fastest.
Arguments:
- queries: bfloat16 [2, 8192, 4096], P(None, 'ctx', 'tsp'), may hold values from -5 to 5
- kv_cache: bfloat16 [2, 8192, 1024], P(None, ('ctx', 'tsp')), may hold values from -5 to 5
- grad_out: bfloat16 [2, 8192, 4096], P(None, 'ctx', 'tsp'), may hold values from -6 to 6
- positions: int32 [8192], P('ctx'), may hold values from 0 to 4095, as said below
Outputs:
- attn_out: bfloat16 [2, 8192, 4096], P(None, 'ctx', 'tsp')
- grad_queries: bfloat16 [2, 8192, 4096], P(None, 'ctx', 'tsp')
- grad_cache: bfloat16 [2, 8192, 1024], P(None, ('ctx', 'tsp'))
Inputs may be any that keep to these rules, and one draw needn't show every extreme that they name: positions[0] = 0, and every later entry is 0 where a document begins or the entry before it plus 1; the sequence holds two to 4 documents.
All inputs are finite; a program needn't handle non-finite values.
Results may differ from a plain program's by a relative error of at most 0.022.
Values may be sent and summed in bfloat16 or wider, within the bound.
A program may use at most 64 MiB of HBM per device.

v0:
```python
import jax
import jax.numpy as jnp
from jax import lax
from jax.sharding import PartitionSpec as P

QUERY_HEADS = 32
KEY_VALUE_HEADS = 8
HEAD_DIMENSION = 128
SHARING_LAYERS = 2
SPAN = 8


def passed_along(shard, axis, by):
    devices = lax.axis_size(axis)
    pairs = [(i, i + by) for i in range(devices) if 0 <= i + by < devices]
    return lax.ppermute(shard, axis, pairs)


def on_device(queries, kv_cache, grad_out, positions):
    row_count = queries.shape[1]
    key_value_width = kv_cache.shape[2] // lax.axis_size("tsp")
    heads_kv = key_value_width // HEAD_DIMENSION
    group_length = QUERY_HEADS // KEY_VALUE_HEADS
    scaling = HEAD_DIMENSION ** (-0.5)
    window = SPAN * row_count
    q_split = queries.reshape(SHARING_LAYERS, row_count, heads_kv, group_length, HEAD_DIMENSION)
    upstream_gradient = grad_out.reshape(
        SHARING_LAYERS, row_count, heads_kv, group_length, HEAD_DIMENSION
    )
    local_kv = lax.all_to_all(kv_cache, "tsp", split_axis=2, concat_axis=1, tiled=True)
    row_index = jnp.arange(row_count, dtype=jnp.int32)
    base_distance = row_index[:, None] - row_index[None, :]

    def scores_for(kv_block, offset):
        key_row_block = kv_block[0].reshape(row_count, heads_kv, HEAD_DIMENSION)
        raw_scores = (
            jnp.einsum(
                "lrkgd,ckd->lkgrc", q_split, key_row_block, preferred_element_type=jnp.float32
            )
            * scaling
        )
        distance = base_distance + offset * row_count
        visible = (distance >= 0) & (distance <= positions[:, None]) & (distance < window)
        return jnp.where(visible, raw_scores, -jnp.inf)

    local_scores = scores_for(local_kv, 0)

    def relay_step(carried, offset):
        arrived = passed_along(carried, "ctx", 1)
        return (arrived, (arrived, scores_for(arrived, offset)))

    offsets = jnp.arange(1, SPAN + 1, dtype=jnp.int32)
    _, (remote, remote_scores) = lax.scan(relay_step, local_kv, offsets)
    blocks = jnp.concatenate([local_kv[None], remote], axis=0)
    scores = jnp.concatenate([local_scores[None], remote_scores], axis=0)
    maxima = jnp.max(scores, axis=(0, 5), keepdims=True)
    expo = jnp.exp(scores - maxima)
    probs = expo / jnp.sum(expo, axis=(0, 5), keepdims=True)
    probs_low = probs.astype(jnp.bfloat16)
    key_blocks = blocks[:, 0].reshape(SPAN + 1, row_count, heads_kv, HEAD_DIMENSION)
    value_blocks = blocks[:, 1].reshape(SPAN + 1, row_count, heads_kv, HEAD_DIMENSION)
    attended = jnp.einsum(
        "blkgrc,bckd->lrkgd", probs_low, value_blocks, preferred_element_type=jnp.float32
    )
    attended_low = attended.astype(jnp.bfloat16)
    delta = jnp.sum(
        upstream_gradient.astype(jnp.float32) * attended_low.astype(jnp.float32), axis=-1
    )
    delta = jnp.transpose(delta, (0, 2, 3, 1))[..., None]

    def block_grads(key_row_block, value_row_block, prob_block, prob_low_block):
        dprobs = jnp.einsum(
            "lrkgd,ckd->lkgrc",
            upstream_gradient,
            value_row_block,
            preferred_element_type=jnp.float32,
        )
        dscores = (prob_block * (dprobs - delta)).astype(jnp.bfloat16)
        query_part = jnp.einsum(
            "lkgrc,ckd->lrkgd", dscores, key_row_block, preferred_element_type=jnp.float32
        )
        key_part = scaling * jnp.einsum(
            "lkgrc,lrkgd->ckd", dscores, q_split, preferred_element_type=jnp.float32
        )
        value_part = jnp.einsum(
            "lkgrc,lrkgd->ckd",
            prob_low_block,
            upstream_gradient,
            preferred_element_type=jnp.float32,
        )
        stacked = jnp.stack(
            [
                key_part.reshape(row_count, key_value_width),
                value_part.reshape(row_count, key_value_width),
            ]
        )
        return (query_part, stacked)

    query_sum, partial_value = block_grads(
        key_blocks[SPAN], value_blocks[SPAN], probs[SPAN], probs_low[SPAN]
    )
    inputs = (
        key_blocks[SPAN - 1 :: -1],
        value_blocks[SPAN - 1 :: -1],
        probs[SPAN - 1 :: -1],
        probs_low[SPAN - 1 :: -1],
    )

    def relay_back(carried, block_inputs):
        query_acc, partial_acc = carried
        arrived = passed_along(partial_acc, "ctx", -1)
        query_part, kv_part = block_grads(
            block_inputs[0], block_inputs[1], block_inputs[2], block_inputs[3]
        )
        return ((query_acc + query_part, arrived + kv_part), None)

    (query_sum, grad_local), _ = lax.scan(relay_back, (query_sum, partial_value), inputs)
    grad_queries = (scaling * query_sum).astype(jnp.bfloat16).reshape(SHARING_LAYERS, row_count, -1)
    grad_cache = lax.all_to_all(
        grad_local.astype(jnp.bfloat16), "tsp", split_axis=1, concat_axis=2, tiled=True
    )
    return (attended_low.reshape(SHARING_LAYERS, row_count, -1), grad_queries, grad_cache)


def solution(mesh):
    return jax.shard_map(
        on_device,
        mesh=mesh,
        in_specs=(
            P(None, "ctx", "tsp"),
            P(None, ("ctx", "tsp"), None),
            P(None, "ctx", "tsp"),
            P("ctx"),
        ),
        out_specs=(P(None, "ctx", "tsp"), P(None, "ctx", "tsp"), P(None, ("ctx", "tsp"), None)),
        check_vma=False,
    )
```

profile of v0, /device:TPU:32, one launch (start us, length us, event | category | flops | bytes accessed | tf_op | source)
XLA Modules:
  0.0 226.5 jit_solution(14002002304505815392)
XLA Ops:
  3.0 4.4 %all-to-all-start = ((bf16[8,2,2048]{2,1,0:T(2,128)(2,1)}), bf16[8,2,2048]{2,1,0:T(2,128)(2,1)S(1)}, u32[]{:S(2)}, u32[]{:S(2)}) async-start(bf16[8,2,2048]{2,1,0:T(2,128)(2,1)} %reshape.267), calls=%async_computation | async-start | bytes 131072 | tf_op jit(solution)/shard_map/all_to_all | solution.py:30
  14.7 88.8 %while.28 = (s32[]{:T(128)}, bf16[2,128,128]{2,1,0:T(8,128)(2,1)S(1)}, bf16[8,2,128,128]{3,2,1,0:T(8,128)(2,1)S(1)}, f32[8,2,1,4,128,128]{4,5,3,1,2,0:T(8,128)},...) while((s32[]{:T(128)}, ...), condition=%wide.region_1.2_spmd.clone, body=%wide.region_0.1_spmd.clone.sunk | while | flops 33931264 | bytes 1376945 | solution.py:53
  17.9 8.4 %collective-permute-done.1 = bf16[2,128,128]{2,1,0:T(8,128)(2,1)S(1)} collective-permute-done((bf16[2,128,128]{2,1,0:T(8,128)(2,1)S(1)}, bf16[2,128,128]{2,1,0:T(8,128)(2,1)S(1)}, u32[]{:S(2)}, u32[]{:S(2)}) %collective-permute-start.1) | collective-permute-done | bytes 65568 | tf_op jit(solution)/shard_map/while/body/eval_jaxpr/ppermute | solution.py:16
  30.6 6.6 %collective-permute-done.1 = bf16[2,128,128]{2,1,0:T(8,128)(2,1)S(1)} collective-permute-done((bf16[2,128,128]{2,1,0:T(8,128)(2,1)S(1)}, bf16[2,128,128]{2,1,0:T(8,128)(2,1)S(1)}, u32[]{:S(2)}, u32[]{:S(2)}) %collective-permute-start.1) | collective-permute-done | bytes 65568 | tf_op jit(solution)/shard_map/while/body/eval_jaxpr/ppermute | solution.py:16
  41.5 6.7 %collective-permute-done.1 = bf16[2,128,128]{2,1,0:T(8,128)(2,1)S(1)} collective-permute-done((bf16[2,128,128]{2,1,0:T(8,128)(2,1)S(1)}, bf16[2,128,128]{2,1,0:T(8,128)(2,1)S(1)}, u32[]{:S(2)}, u32[]{:S(2)}) %collective-permute-start.1) | collective-permute-done | bytes 65568 | tf_op jit(solution)/shard_map/while/body/eval_jaxpr/ppermute | solution.py:16
  52.4 6.6 %collective-permute-done.1 = bf16[2,128,128]{2,1,0:T(8,128)(2,1)S(1)} collective-permute-done((bf16[2,128,128]{2,1,0:T(8,128)(2,1)S(1)}, bf16[2,128,128]{2,1,0:T(8,128)(2,1)S(1)}, u32[]{:S(2)}, u32[]{:S(2)}) %collective-permute-start.1) | collective-permute-done | bytes 65568 | tf_op jit(solution)/shard_map/while/body/eval_jaxpr/ppermute | solution.py:16
  63.3 6.6 %collective-permute-done.1 = bf16[2,128,128]{2,1,0:T(8,128)(2,1)S(1)} collective-permute-done((bf16[2,128,128]{2,1,0:T(8,128)(2,1)S(1)}, bf16[2,128,128]{2,1,0:T(8,128)(2,1)S(1)}, u32[]{:S(2)}, u32[]{:S(2)}) %collective-permute-start.1) | collective-permute-done | bytes 65568 | tf_op jit(solution)/shard_map/while/body/eval_jaxpr/ppermute | solution.py:16
  74.1 6.6 %collective-permute-done.1 = bf16[2,128,128]{2,1,0:T(8,128)(2,1)S(1)} collective-permute-done((bf16[2,128,128]{2,1,0:T(8,128)(2,1)S(1)}, bf16[2,128,128]{2,1,0:T(8,128)(2,1)S(1)}, u32[]{:S(2)}, u32[]{:S(2)}) %collective-permute-start.1) | collective-permute-done | bytes 65568 | tf_op jit(solution)/shard_map/while/body/eval_jaxpr/ppermute | solution.py:16
  85.0 6.6 %collective-permute-done.1 = bf16[2,128,128]{2,1,0:T(8,128)(2,1)S(1)} collective-permute-done((bf16[2,128,128]{2,1,0:T(8,128)(2,1)S(1)}, bf16[2,128,128]{2,1,0:T(8,128)(2,1)S(1)}, u32[]{:S(2)}, u32[]{:S(2)}) %collective-permute-start.1) | collective-permute-done | bytes 65568 | tf_op jit(solution)/shard_map/while/body/eval_jaxpr/ppermute | solution.py:16
  95.9 6.6 %collective-permute-done.1 = bf16[2,128,128]{2,1,0:T(8,128)(2,1)S(1)} collective-permute-done((bf16[2,128,128]{2,1,0:T(8,128)(2,1)S(1)}, bf16[2,128,128]{2,1,0:T(8,128)(2,1)S(1)}, u32[]{:S(2)}, u32[]{:S(2)}) %collective-permute-start.1) | collective-permute-done | bytes 65568 | tf_op jit(solution)/shard_map/while/body/eval_jaxpr/ppermute | solution.py:16
  108.3 3.0 %fusion.34 = f32[2,4,128]{2,1,0:T(4,128)S(1)} fusion(f32[8,2,1,4,128,128]{4,5,3,1,2,0:T(8,128)} %get-tuple-element.100, f32[1,2,1,4,128,128]{4,5,3,1,2,0:T(8,128)S(1)} %bitcast.318, f32[2,4,128]{2,1,0:T(4,128)S(1)} %reduce_max.22), kind=kLoop, calls=%fused_computation.46 | loop fusion | flops 3537920 | bytes 4726784 | tf_op jit(solution)/shard_map/reduce_sum | solution.py:58
  111.5 3.1 %fusion.76 = (bf16[9,2,1,4,128,128]{4,5,3,1,2,0:T(8,128)(2,1)S(1)}, f32[9,2,1,4,128,128]{4,5,3,1,2,0:T(8,128)}) fusion(f32[2,4,128]{2,1,0:T(4,128)S(1)} %fusion.34, f32[2,4,128]{2,1,0:T(4,128)S(1)} %reduce_max.22, f32[8,2,1,4,128,128]{4,5,3,1,2,0:T(8,128)S(1)} %copy-done, f32[1,2,1,4,128,128]{4,5,3,1,2,0:T(8,128)S(1)} %bitcast.319), kind=kLoop, calls=%fused_computation.102 | loop fusion | flops 4718592 | bytes 11804672 | tf_op jit(solution)/shard_map/convert_element_type | solution.py:59
  115.8 4.9 %slice.71 = f32[8,2,1,4,128,128]{4,5,3,1,2,0:T(8,128)} slice(f32[9,2,1,4,128,128]{4,5,3,1,2,0:T(8,128)} %get-tuple-element.247), slice={[0:8], [0:2], [0:1], [0:4], [0:128], [0:128]} | slice | bytes 8388608 | tf_op jit(solution)/shard_map/slice | solution.py:105
  125.7 4.6 %rev.13 = f32[8,2,1,4,128,128]{4,5,3,1,2,0:T(8,128)} reverse(f32[8,2,1,4,128,128]{4,5,3,1,2,0:T(8,128)} %slice.71), dimensions={0} | reverse | bytes 8388608 | tf_op jit(solution)/shard_map/rev | solution.py:105
  132.9 82.5 %while.27 = (s32[]{:T(128)}, f32[2,128,1,4,128]{1,4,3,0,2:T(8,128)S(1)}, f32[2,128,128]{2,1,0:T(8,128)S(1)}, bf16[8,128,1,128]{1,3,2,0:T(8,128)(2,1)S(1)}, f32[8...) while((s32[]{:T(128)}, ...), condition=%wide.region_7.8_spmd, body=%wide.region_6.7_spmd.sunk | while | flops 134823936 | bytes 4527269 | solution.py:117
  138.9 8.0 %collective-permute-start = (f32[2,128,128]{2,1,0:T(8,128)S(1)}, f32[2,128,128]{2,1,0:T(8,128)S(1)}, u32[]{:S(2)}, u32[]{:S(2)}) collective-permute-start(f32[2,128,128]{2,1,0:T(8,128)S(1)} %get-tuple-element.398), channel_id=1, source_target_pairs={{8,0},{16,8},{24,16},{32,24},{40,32},{48,40},{56,48},{64,56},{72,6... | collective-permute-start | bytes 393224 | tf_op jit(solution)/shard_map/while/body/eval_jaxpr/ppermute | solution.py:16
  149.9 7.8 %collective-permute-start = (f32[2,128,128]{2,1,0:T(8,128)S(1)}, f32[2,128,128]{2,1,0:T(8,128)S(1)}, u32[]{:S(2)}, u32[]{:S(2)}) collective-permute-start(f32[2,128,128]{2,1,0:T(8,128)S(1)} %get-tuple-element.398), channel_id=1, source_target_pairs={{8,0},{16,8},{24,16},{32,24},{40,32},{48,40},{56,48},{64,56},{72,6... | collective-permute-start | bytes 393224 | tf_op jit(solution)/shard_map/while/body/eval_jaxpr/ppermute | solution.py:16
  160.9 8.0 %collective-permute-start = (f32[2,128,128]{2,1,0:T(8,128)S(1)}, f32[2,128,128]{2,1,0:T(8,128)S(1)}, u32[]{:S(2)}, u32[]{:S(2)}) collective-permute-start(f32[2,128,128]{2,1,0:T(8,128)S(1)} %get-tuple-element.398), channel_id=1, source_target_pairs={{8,0},{16,8},{24,16},{32,24},{40,32},{48,40},{56,48},{64,56},{72,6... | collective-permute-start | bytes 393224 | tf_op jit(solution)/shard_map/while/body/eval_jaxpr/ppermute | solution.py:16
  172.3 8.1 %collective-permute-start = (f32[2,128,128]{2,1,0:T(8,128)S(1)}, f32[2,128,128]{2,1,0:T(8,128)S(1)}, u32[]{:S(2)}, u32[]{:S(2)}) collective-permute-start(f32[2,128,128]{2,1,0:T(8,128)S(1)} %get-tuple-element.398), channel_id=1, source_target_pairs={{8,0},{16,8},{24,16},{32,24},{40,32},{48,40},{56,48},{64,56},{72,6... | collective-permute-start | bytes 393224 | tf_op jit(solution)/shard_map/while/body/eval_jaxpr/ppermute | solution.py:16
  183.5 7.6 %collective-permute-start = (f32[2,128,128]{2,1,0:T(8,128)S(1)}, f32[2,128,128]{2,1,0:T(8,128)S(1)}, u32[]{:S(2)}, u32[]{:S(2)}) collective-permute-start(f32[2,128,128]{2,1,0:T(8,128)S(1)} %get-tuple-element.398), channel_id=1, source_target_pairs={{8,0},{16,8},{24,16},{32,24},{40,32},{48,40},{56,48},{64,56},{72,6... | collective-permute-start | bytes 393224 | tf_op jit(solution)/shard_map/while/body/eval_jaxpr/ppermute | solution.py:16
  194.1 7.6 %collective-permute-start = (f32[2,128,128]{2,1,0:T(8,128)S(1)}, f32[2,128,128]{2,1,0:T(8,128)S(1)}, u32[]{:S(2)}, u32[]{:S(2)}) collective-permute-start(f32[2,128,128]{2,1,0:T(8,128)S(1)} %get-tuple-element.398), channel_id=1, source_target_pairs={{8,0},{16,8},{24,16},{32,24},{40,32},{48,40},{56,48},{64,56},{72,6... | collective-permute-start | bytes 393224 | tf_op jit(solution)/shard_map/while/body/eval_jaxpr/ppermute | solution.py:16
  204.7 7.6 %collective-permute-start = (f32[2,128,128]{2,1,0:T(8,128)S(1)}, f32[2,128,128]{2,1,0:T(8,128)S(1)}, u32[]{:S(2)}, u32[]{:S(2)}) collective-permute-start(f32[2,128,128]{2,1,0:T(8,128)S(1)} %get-tuple-element.398), channel_id=1, source_target_pairs={{8,0},{16,8},{24,16},{32,24},{40,32},{48,40},{56,48},{64,56},{72,6... | collective-permute-start | bytes 393224 | tf_op jit(solution)/shard_map/while/body/eval_jaxpr/ppermute | solution.py:16
  216.1 3.4 %all-to-all-start.1 = ((bf16[2,128,128]{2,0,1:T(2,128)(2,1)}), bf16[2,128,128]{2,0,1:T(2,128)(2,1)S(1)}, u32[]{:S(2)}, u32[]{:S(2)}) async-start(bf16[2,128,128]{2,0,1:T(2,128)(2,1)} %copy.195), calls=%async_computation.1 | async-start | bytes 131072 | tf_op jit(solution)/shard_map/all_to_all | solution.py:119
  221.2 4.6 %all-to-all-done.1 = bf16[2,128,128]{2,0,1:T(2,128)(2,1)S(1)} async-done(((bf16[2,128,128]{2,0,1:T(2,128)(2,1)}), bf16[2,128,128]{2,0,1:T(2,128)(2,1)S(1)}, u32[]{:S(2)}, u32[]{:S(2)}) %all-to-all-start.1) | async-done | bytes 65568 | tf_op jit(solution)/shard_map/all_to_all | solution.py:119
  (164 shorter events, 82.2 us)
Async XLA Ops:
  0.6 14.1 %copy-start.12 = (s32[128]{0:T(128)S(1)}, s32[128]{0:T(128)}, u32[]{:S(2)}) copy-start(s32[128]{0:T(128)} %param.11) | copy-start | bytes 1540
  3.0 10.8 %all-to-all-start = ((bf16[8,2,2048]{2,1,0:T(2,128)(2,1)}), bf16[8,2,2048]{2,1,0:T(2,128)(2,1)S(1)}, u32[]{:S(2)}, u32[]{:S(2)}) async-start(bf16[8,2,2048]{2,1,0:T(2,128)(2,1)} %reshape.267), calls=%async_computation | async-start | bytes 131072 | tf_op jit(solution)/shard_map/all_to_all | solution.py:30
  14.7 11.6 %collective-permute-start.1 = (bf16[2,128,128]{2,1,0:T(8,128)(2,1)S(1)}, bf16[2,128,128]{2,1,0:T(8,128)(2,1)S(1)}, u32[]{:S(2)}, u32[]{:S(2)}) collective-permute-start(bf16[2,128,128]{2,1,0:T(8,128)(2,1)S(1)} %get-tuple-element.368), channel_id=1, source_target_pairs={{0,8},{8,16},{16,24},{24,32},{32,40},{40,48},{48,56},{56,64},{64,7... | collective-permute-start | bytes 196616 | tf_op jit(solution)/shard_map/while/body/eval_jaxpr/ppermute | solution.py:16
  27.4 9.8 %collective-permute-start.1 = (bf16[2,128,128]{2,1,0:T(8,128)(2,1)S(1)}, bf16[2,128,128]{2,1,0:T(8,128)(2,1)S(1)}, u32[]{:S(2)}, u32[]{:S(2)}) collective-permute-start(bf16[2,128,128]{2,1,0:T(8,128)(2,1)S(1)} %get-tuple-element.368), channel_id=1, source_target_pairs={{0,8},{8,16},{16,24},{24,32},{32,40},{40,48},{48,56},{56,64},{64,7... | collective-permute-start | bytes 196616 | tf_op jit(solution)/shard_map/while/body/eval_jaxpr/ppermute | solution.py:16
  38.3 9.9 %collective-permute-start.1 = (bf16[2,128,128]{2,1,0:T(8,128)(2,1)S(1)}, bf16[2,128,128]{2,1,0:T(8,128)(2,1)S(1)}, u32[]{:S(2)}, u32[]{:S(2)}) collective-permute-start(bf16[2,128,128]{2,1,0:T(8,128)(2,1)S(1)} %get-tuple-element.368), channel_id=1, source_target_pairs={{0,8},{8,16},{16,24},{24,32},{32,40},{40,48},{48,56},{56,64},{64,7... | collective-permute-start | bytes 196616 | tf_op jit(solution)/shard_map/while/body/eval_jaxpr/ppermute | solution.py:16
  49.2 9.8 %collective-permute-start.1 = (bf16[2,128,128]{2,1,0:T(8,128)(2,1)S(1)}, bf16[2,128,128]{2,1,0:T(8,128)(2,1)S(1)}, u32[]{:S(2)}, u32[]{:S(2)}) collective-permute-start(bf16[2,128,128]{2,1,0:T(8,128)(2,1)S(1)} %get-tuple-element.368), channel_id=1, source_target_pairs={{0,8},{8,16},{16,24},{24,32},{32,40},{40,48},{48,56},{56,64},{64,7... | collective-permute-start | bytes 196616 | tf_op jit(solution)/shard_map/while/body/eval_jaxpr/ppermute | solution.py:16
  60.1 9.8 %collective-permute-start.1 = (bf16[2,128,128]{2,1,0:T(8,128)(2,1)S(1)}, bf16[2,128,128]{2,1,0:T(8,128)(2,1)S(1)}, u32[]{:S(2)}, u32[]{:S(2)}) collective-permute-start(bf16[2,128,128]{2,1,0:T(8,128)(2,1)S(1)} %get-tuple-element.368), channel_id=1, source_target_pairs={{0,8},{8,16},{16,24},{24,32},{32,40},{40,48},{48,56},{56,64},{64,7... | collective-permute-start | bytes 196616 | tf_op jit(solution)/shard_map/while/body/eval_jaxpr/ppermute | solution.py:16
  70.9 9.8 %collective-permute-start.1 = (bf16[2,128,128]{2,1,0:T(8,128)(2,1)S(1)}, bf16[2,128,128]{2,1,0:T(8,128)(2,1)S(1)}, u32[]{:S(2)}, u32[]{:S(2)}) collective-permute-start(bf16[2,128,128]{2,1,0:T(8,128)(2,1)S(1)} %get-tuple-element.368), channel_id=1, source_target_pairs={{0,8},{8,16},{16,24},{24,32},{32,40},{40,48},{48,56},{56,64},{64,7... | collective-permute-start | bytes 196616 | tf_op jit(solution)/shard_map/while/body/eval_jaxpr/ppermute | solution.py:16
  81.8 9.8 %collective-permute-start.1 = (bf16[2,128,128]{2,1,0:T(8,128)(2,1)S(1)}, bf16[2,128,128]{2,1,0:T(8,128)(2,1)S(1)}, u32[]{:S(2)}, u32[]{:S(2)}) collective-permute-start(bf16[2,128,128]{2,1,0:T(8,128)(2,1)S(1)} %get-tuple-element.368), channel_id=1, source_target_pairs={{0,8},{8,16},{16,24},{24,32},{32,40},{40,48},{48,56},{56,64},{64,7... | collective-permute-start | bytes 196616 | tf_op jit(solution)/shard_map/while/body/eval_jaxpr/ppermute | solution.py:16
  92.7 9.8 %collective-permute-start.1 = (bf16[2,128,128]{2,1,0:T(8,128)(2,1)S(1)}, bf16[2,128,128]{2,1,0:T(8,128)(2,1)S(1)}, u32[]{:S(2)}, u32[]{:S(2)}) collective-permute-start(bf16[2,128,128]{2,1,0:T(8,128)(2,1)S(1)} %get-tuple-element.368), channel_id=1, source_target_pairs={{0,8},{8,16},{16,24},{24,32},{32,40},{40,48},{48,56},{56,64},{64,7... | collective-permute-start | bytes 196616 | tf_op jit(solution)/shard_map/while/body/eval_jaxpr/ppermute | solution.py:16
  103.5 7.8 %copy-start.2 = (bf16[8,2,128,128]{3,2,1,0:T(8,128)(2,1)}, bf16[8,2,128,128]{3,2,1,0:T(8,128)(2,1)S(1)}, u32[]{:S(2)}) copy-start(bf16[8,2,128,128]{3,2,1,0:T(8,128)(2,1)S(1)} %get-tuple-element.99) | copy-start | bytes 1572868
  115.7 4.9 %copy-start.3 = (bf16[8,2,128,128]{2,3,0,1:T(8,128)(2,1)S(1)}, bf16[8,2,128,128]{2,3,0,1:T(8,128)(2,1)}, u32[]{:S(2)}) copy-start(bf16[8,2,128,128]{2,3,0,1:T(8,128)(2,1)} %copy.121) | copy-start | bytes 1572868
  115.7 5.7 %copy-start.1 = (f32[8,2,1,4,128,128]{4,5,3,1,2,0:T(8,128)S(1)}, f32[8,2,1,4,128,128]{4,5,3,1,2,0:T(8,128)}, u32[]{:S(2)}) copy-start(f32[8,2,1,4,128,128]{4,5,3,1,2,0:T(8,128)} %get-tuple-element.100) | copy-start | bytes 12582916
  115.7 5.7 %copy-start.7 = (bf16[2,128,512]{1,2,0:T(8,128)(2,1)S(1)}, bf16[2,128,512]{1,2,0:T(8,128)(2,1)}, u32[]{:S(2)}) copy-start(bf16[2,128,512]{1,2,0:T(8,128)(2,1)} %copy-done.6) | copy-start | bytes 786436
  132.9 87.5 %copy-start.10 = (bf16[128,2,4,128]{3,0,2,1:T(8,128)(2,1)S(1)}, bf16[128,2,4,128]{3,0,2,1:T(8,128)(2,1)}, u32[]{:S(2)}) copy-start(bf16[128,2,4,128]{3,0,2,1:T(8,128)(2,1)} %get-tuple-element.253) | copy-start | bytes 786436
  132.9 6.0 %collective-permute-start = (f32[2,128,128]{2,1,0:T(8,128)S(1)}, f32[2,128,128]{2,1,0:T(8,128)S(1)}, u32[]{:S(2)}, u32[]{:S(2)}) collective-permute-start(f32[2,128,128]{2,1,0:T(8,128)S(1)} %get-tuple-element.398), channel_id=1, source_target_pairs={{8,0},{16,8},{24,16},{32,24},{40,32},{48,40},{56,48},{64,56},{72,6... | collective-permute-start | bytes 393224 | tf_op jit(solution)/shard_map/while/body/eval_jaxpr/ppermute | solution.py:16
  138.9 11.0 %collective-permute-start = (f32[2,128,128]{2,1,0:T(8,128)S(1)}, f32[2,128,128]{2,1,0:T(8,128)S(1)}, u32[]{:S(2)}, u32[]{:S(2)}) collective-permute-start(f32[2,128,128]{2,1,0:T(8,128)S(1)} %get-tuple-element.398), channel_id=1, source_target_pairs={{8,0},{16,8},{24,16},{32,24},{40,32},{48,40},{56,48},{64,56},{72,6... | collective-permute-start | bytes 393224 | tf_op jit(solution)/shard_map/while/body/eval_jaxpr/ppermute | solution.py:16
  149.9 11.0 %collective-permute-start = (f32[2,128,128]{2,1,0:T(8,128)S(1)}, f32[2,128,128]{2,1,0:T(8,128)S(1)}, u32[]{:S(2)}, u32[]{:S(2)}) collective-permute-start(f32[2,128,128]{2,1,0:T(8,128)S(1)} %get-tuple-element.398), channel_id=1, source_target_pairs={{8,0},{16,8},{24,16},{32,24},{40,32},{48,40},{56,48},{64,56},{72,6... | collective-permute-start | bytes 393224 | tf_op jit(solution)/shard_map/while/body/eval_jaxpr/ppermute | solution.py:16
  160.9 11.3 %collective-permute-start = (f32[2,128,128]{2,1,0:T(8,128)S(1)}, f32[2,128,128]{2,1,0:T(8,128)S(1)}, u32[]{:S(2)}, u32[]{:S(2)}) collective-permute-start(f32[2,128,128]{2,1,0:T(8,128)S(1)} %get-tuple-element.398), channel_id=1, source_target_pairs={{8,0},{16,8},{24,16},{32,24},{40,32},{48,40},{56,48},{64,56},{72,6... | collective-permute-start | bytes 393224 | tf_op jit(solution)/shard_map/while/body/eval_jaxpr/ppermute | solution.py:16
  172.3 11.1 %collective-permute-start = (f32[2,128,128]{2,1,0:T(8,128)S(1)}, f32[2,128,128]{2,1,0:T(8,128)S(1)}, u32[]{:S(2)}, u32[]{:S(2)}) collective-permute-start(f32[2,128,128]{2,1,0:T(8,128)S(1)} %get-tuple-element.398), channel_id=1, source_target_pairs={{8,0},{16,8},{24,16},{32,24},{40,32},{48,40},{56,48},{64,56},{72,6... | collective-permute-start | bytes 393224 | tf_op jit(solution)/shard_map/while/body/eval_jaxpr/ppermute | solution.py:16
  183.5 10.6 %collective-permute-start = (f32[2,128,128]{2,1,0:T(8,128)S(1)}, f32[2,128,128]{2,1,0:T(8,128)S(1)}, u32[]{:S(2)}, u32[]{:S(2)}) collective-permute-start(f32[2,128,128]{2,1,0:T(8,128)S(1)} %get-tuple-element.398), channel_id=1, source_target_pairs={{8,0},{16,8},{24,16},{32,24},{40,32},{48,40},{56,48},{64,56},{72,6... | collective-permute-start | bytes 393224 | tf_op jit(solution)/shard_map/while/body/eval_jaxpr/ppermute | solution.py:16
  194.1 10.6 %collective-permute-start = (f32[2,128,128]{2,1,0:T(8,128)S(1)}, f32[2,128,128]{2,1,0:T(8,128)S(1)}, u32[]{:S(2)}, u32[]{:S(2)}) collective-permute-start(f32[2,128,128]{2,1,0:T(8,128)S(1)} %get-tuple-element.398), channel_id=1, source_target_pairs={{8,0},{16,8},{24,16},{32,24},{40,32},{48,40},{56,48},{64,56},{72,6... | collective-permute-start | bytes 393224 | tf_op jit(solution)/shard_map/while/body/eval_jaxpr/ppermute | solution.py:16
  204.7 10.6 %collective-permute-start = (f32[2,128,128]{2,1,0:T(8,128)S(1)}, f32[2,128,128]{2,1,0:T(8,128)S(1)}, u32[]{:S(2)}, u32[]{:S(2)}) collective-permute-start(f32[2,128,128]{2,1,0:T(8,128)S(1)} %get-tuple-element.398), channel_id=1, source_target_pairs={{8,0},{16,8},{24,16},{32,24},{40,32},{48,40},{56,48},{64,56},{72,6... | collective-permute-start | bytes 393224 | tf_op jit(solution)/shard_map/while/body/eval_jaxpr/ppermute | solution.py:16
  216.1 9.7 %all-to-all-start.1 = ((bf16[2,128,128]{2,0,1:T(2,128)(2,1)}), bf16[2,128,128]{2,0,1:T(2,128)(2,1)S(1)}, u32[]{:S(2)}, u32[]{:S(2)}) async-start(bf16[2,128,128]{2,0,1:T(2,128)(2,1)} %copy.195), calls=%async_computation.1 | async-start | bytes 131072 | tf_op jit(solution)/shard_map/all_to_all | solution.py:119
  (7 other events, 18.5 us)
where the time goes:
time: 228 us; the launch traced here: 226 us
  starting transfers between devices  79.9 us (35%)
  waiting for transfers between devices  63.1 us (28%)
  matrix products  37.1 us (16%)
  local copies, waits for them, and re-layouts  29 us (13%)
  other arithmetic  10.5 us (5%)
  loops' own time  5.87 us (3%)
    ppermute x16, starting transfers between devices, passed_along(): return lax.ppermute(shard, axis, pairs)  72.2 us
    ppermute x16, waiting for transfers between devices, passed_along(): return lax.ppermute(shard, axis, pairs)  56.3 us
    dot_general x9, matrix products, block_grads(): jnp.einsum('lrkgd,ckd->lkgrc', upstream_gradient, value_row_block, prefer...  11.7 us
    dot_general x9, matrix products, block_grads(): jnp.einsum('lkgrc,lrkgd->ckd', prob_low_block, upstream_gradient, preferr...  10.2 us
    dot_general x9, matrix products, scores_for(): jnp.einsum('lrkgd,ckd->lkgrc', q_split, key_row_block, preferred_element_...  8.6 us
    unnamed x34, local copies, waits for them, and re-layouts  6.69 us
    another operation x1, loops' own time, on_device(): _, (remote, remote_scores) = lax.scan(relay_step, local_kv, offsets)  5.36 us
    slice x1, local copies, waits for them, and re-layouts, on_device(): probs[SPAN - 1::-1]  4.86 us
  transfers between devices with their start and end apart: 18, of which 13 were waited for; matrix products, arithmetic and copies ran while one was open for 15% of the time, Pallas kernels for 0%

commit v1 on v0

v1 whole, which is shorter than its diff:
```python
import functools
import math

import jax
import jax.numpy as jnp
from jax import lax
from jax.experimental import pallas as pl
from jax.experimental.pallas import tpu as pltpu
from jax.sharding import PartitionSpec as P

LAYERS = 2
GROUP = 4
DIM = 128
ROWS = 128
SPAN = 8
NEAR = SPAN // 2
SLOTS = SPAN + 1
HEADS = LAYERS * GROUP
COLS = HEADS * ROWS
CHUNK = 256
SCALE = DIM ** (-0.5)
TO_EXP2 = SCALE * math.log2(math.e)
LOW = -1e30
MESH = pl.DeviceIdType.MESH
F32 = jnp.float32
BF16 = jnp.bfloat16


def dot(a, b):
    return lax.dot_general(a, b, (((1,), (0,)), ((), ())), preferred_element_type=F32)


def kernel(
    blocks, lanes,
    q_hbm, kv_hbm, g_hbm, pos_ref,
    o_hbm, dq_hbm, dkv_ref,
    kv, qs, gs, q_t, g_t, keys, vals, k_t, v_t, bias,
    top, total, tops, expo, probs, dprobs, dscores, delta, o_acc,
    pair_out, pair_in, ready, landed, o_out, dq_out,
    in_sem, out_sem, kv_send, kv_recv, pair_send, pair_recv,
    back_send, back_recv, swap_send, swap_recv,
):
    c = lax.axis_index("ctx")
    t = lax.axis_index("tsp")
    core = lax.rem(c, 2)
    partner = (c + 1 - 2 * core, t)
    piece = ROWS // lanes

    def lane(i):
        return lax.rem(t + i, lanes)

    def ahead(d):
        return lax.rem(c + 2 * d, blocks)

    def behind(d):
        return lax.rem(c + blocks - 2 * d, blocks)

    barrier = pltpu.get_barrier_semaphore()
    pl.semaphore_signal(barrier, inc=1, device_id=partner, device_id_type=MESH)
    for d in range(NEAR + 1):
        def hello(i, _, d=d):
            pl.semaphore_signal(barrier, inc=1, device_id=(behind(d), lane(i)), device_id_type=MESH)
            return 0
        lax.fori_loop(1 if d == 0 else 0, lanes, hello, 0)

    kv_copy = pltpu.make_async_copy(kv_hbm, kv, in_sem.at[0])
    kv_copy.start()
    def loads():
        out = []
        for l in range(LAYERS):
            for g in range(GROUP):
                n = l * GROUP + g
                cut = pl.ds(g * DIM, DIM)
                out.append(pltpu.make_async_copy(q_hbm.at[l, :, cut], qs.at[pl.ds(n * ROWS, ROWS)], in_sem.at[1 + n]))
                out.append(pltpu.make_async_copy(g_hbm.at[l, :, cut], gs.at[pl.ds(n * ROWS, ROWS)], in_sem.at[1 + HEADS + n]))
        return out
    for copy in loads():
        copy.start()
    kv_copy.wait()
    pl.semaphore_wait(barrier, (NEAR + 1) * lanes)

    def kv_piece(kind, d, i):
        to = lane(i)
        place = (keys if kind == 0 else vals)
        return pltpu.make_async_remote_copy(
            kv.at[kind, :, pl.ds(pl.multiple_of(to * DIM, DIM), DIM)],
            place.at[2 * d, pl.ds(pl.multiple_of(t * piece, piece), piece)],
            kv_send.at[kind, d],
            kv_recv.at[kind, d],
            device_id=(ahead(d), to),
            device_id_type=MESH,
        )
    def own_piece(kind):
        place = (keys if kind == 0 else vals)
        return pltpu.make_async_copy(
            kv.at[kind, :, pl.ds(pl.multiple_of(t * DIM, DIM), DIM)],
            place.at[0, pl.ds(pl.multiple_of(t * piece, piece), piece)],
            in_sem.at[1 + 2 * HEADS + kind],
        )
    for kind in range(2):
        own_piece(kind).start()
        for d in range(NEAR + 1):
            def send(i, _, kind=kind, d=d):
                kv_piece(kind, d, i).start()
                return 0
            lax.fori_loop(1 if d == 0 else 0, lanes, send, 0)

    def whole(buf, kind, d, rows=ROWS):
        return pltpu.make_async_remote_copy(
            buf.at[0, pl.ds(0, rows)], buf.at[0, pl.ds(0, rows)],
            kv_send.at[kind, d], kv_recv.at[kind, d],
            device_id=partner, device_id_type=MESH,
        )
    def relay(kind, d):
        place = (keys if kind == 0 else vals)
        e = d - core
        return pltpu.make_async_remote_copy(
            place.at[2 * d], place.at[2 * e + 1],
            pair_send.at[kind, e], pair_recv.at[kind, e],
            device_id=partner, device_id_type=MESH,
        )
    def relayed(kind, e):
        place = (keys if kind == 0 else vals)
        return pltpu.make_async_remote_copy(
            place.at[2 * (e + core)], place.at[2 * e + 1],
            pair_send.at[kind, e], pair_recv.at[kind, e],
            device_id=partner, device_id_type=MESH,
        )

    for copy in loads():
        copy.wait()
    for n in range(HEADS):
        part = pl.ds(n * ROWS, ROWS)
        q_t[:, part] = qs[part].T
        g_t[:, part] = gs[part].T
    pos = pos_ref[...]
    base = lax.broadcasted_iota(jnp.int32, (ROWS, ROWS), 1) - lax.broadcasted_iota(jnp.int32, (ROWS, ROWS), 0)
    def mask(o, _):
        distance = base + o * ROWS
        visible = (distance >= 0) & (distance <= pos) & (distance < SPAN * ROWS)
        bias[o] = jnp.where(visible, 0.0, -jnp.inf)
        return 0
    lax.fori_loop(0, SLOTS, mask, 0)
    top[...] = jnp.full(top.shape, LOW, F32)
    total[...] = jnp.zeros(total.shape, F32)

    def chunks():
        return [pl.ds(i * CHUNK, CHUNK) for i in range(COLS // CHUNK)]

    def rows_of(o):
        if isinstance(o, int):
            return pl.ds(o * ROWS, ROWS)
        return pl.ds(pl.multiple_of(o * ROWS, ROWS), ROWS)

    def score(o):
        block = keys[o]
        hide = jnp.concatenate([bias[o]] * (CHUNK // ROWS), axis=1)
        for cut in chunks():
            s = dot(block, q_t[:, cut]) + hide
            before = top[:, cut]
            now = jnp.maximum(before, jnp.max(s, axis=0, keepdims=True))
            e = jnp.exp2((s - now) * TO_EXP2)
            total[:, cut] = total[:, cut] * jnp.exp2((before - now) * TO_EXP2) + jnp.sum(e, axis=0, keepdims=True)
            top[:, cut] = now
            tops[o, :, cut] = now
            expo[rows_of(o), cut] = e
        k_t[:, rows_of(o)] = block.T

    def value(o):
        block = vals[o]
        for cut in chunks():
            dprobs[rows_of(o), cut] = dot(block, g_t[:, cut])
        v_t[:, rows_of(o)] = block.T

    def gather(kind, use):
        own_piece(kind).wait()
        whole((keys if kind == 0 else vals), kind, 0, ROWS - piece).wait_recv()
        @pl.when(core == 0)
        def _():
            relay(kind, 0).start()
        use(0)
        def step(d, _):
            whole((keys if kind == 0 else vals), kind, d).wait_recv()
            @pl.when(d - core < NEAR)
            def _():
                relay(kind, d).start()
            use(2 * d)
            relayed(kind, d - 1).wait_recv()
            use(2 * d - 1)
            return 0
        lax.fori_loop(1, NEAR + 1, step, 0)

    gather(0, score)

    def factor(o, cut):
        return tops[o, :, cut]

    inverse = 1.0 / total[...]
    last = top[...]
    def scales(o, _):
        tops[o] = jnp.exp2((tops[o] - last) * TO_EXP2) * inverse
        return 0
    lax.fori_loop(0, SLOTS, scales, 0)
    def soft(o, _):
        for cut in chunks():
            probs[rows_of(o), cut] = (expo[rows_of(o), cut] * factor(o, cut)).astype(BF16)
        return 0
    lax.fori_loop(0, SLOTS, soft, 0)

    def swap(kind, e):
        return pltpu.make_async_remote_copy(
            pair_out.at[kind, e], pair_in.at[kind, e],
            swap_send.at[kind, e], swap_recv.at[kind, e],
            device_id=partner, device_id_type=MESH,
        )
    def back_piece(kind, d, i):
        to = lane(i)
        return pltpu.make_async_remote_copy(
            ready.at[kind, d, pl.ds(pl.multiple_of(to * piece, piece), piece)],
            landed.at[kind, d, t],
            back_send.at[kind, d],
            back_recv.at[kind, d],
            device_id=(behind(d), to),
            device_id_type=MESH,
        )
    def give_back(kind, left, right):
        def odd(i, _):
            e = NEAR - 1 - i
            pair_out[kind, e] = dot(left[rows_of(2 * e + 1), :], right[...])
            swap(kind, e).start()
            return 0
        lax.fori_loop(0, NEAR, odd, 0)
        def even(i, _):
            d = NEAR - i
            mine = dot(left[rows_of(2 * d), :], right[...])
            e = d - core
            paired = (e >= 0) & (e < NEAR)
            @pl.when(paired)
            def _():
                swap(kind, e).wait_recv()
                both = mine + pair_in[kind, e]
                ready[kind, d] = (both if kind == 1 else both * SCALE).astype(BF16)
            @pl.when(jnp.logical_not(paired))
            def _():
                ready[kind, d] = (mine if kind == 1 else mine * SCALE).astype(BF16)
            def send(i, _):
                back_piece(kind, d, i).start()
                return 0
            lax.fori_loop(jnp.where(d == 0, 1, 0), lanes, send, 0)
            return 0
        lax.fori_loop(0, NEAR + 1, even, 0)
        landed[kind, 0, t] = ready[kind, 0, pl.ds(pl.multiple_of(t * piece, piece), piece), :]

    give_back(1, probs, gs)

    gather(1, value)

    for i, cut in enumerate(chunks()):
        o = dot(v_t[...], probs[:, cut]).astype(BF16)
        o_acc[:, cut] = o
        delta[:, cut] = jnp.sum(o.astype(F32) * g_t[:, cut].astype(F32), axis=0, keepdims=True)

    def soft_back(o, _):
        for cut in chunks():
            p = expo[rows_of(o), cut] * factor(o, cut)
            dscores[rows_of(o), cut] = (p * (dprobs[rows_of(o), cut] - delta[:, cut])).astype(BF16)
        return 0
    lax.fori_loop(0, SLOTS, soft_back, 0)

    give_back(0, dscores, qs)

    for n in range(HEADS):
        l, g = n // GROUP, n % GROUP
        part = pl.ds(n * ROWS, ROWS)
        o_out[l, :, pl.ds(g * DIM, DIM)] = o_acc[:, part].T
    o_copy = pltpu.make_async_copy(o_out, o_hbm, out_sem.at[0])
    o_copy.start()
    for i, cut in enumerate(chunks()):
        dq = (dot(k_t[...], dscores[:, cut]) * SCALE).astype(BF16)
        for j in range(CHUNK // ROWS):
            n = i * (CHUNK // ROWS) + j
            l, g = n // GROUP, n % GROUP
            dq_out[l, :, pl.ds(g * DIM, DIM)] = dq[:, j * ROWS:(j + 1) * ROWS].T
    dq_copy = pltpu.make_async_copy(dq_out, dq_hbm, out_sem.at[1])
    dq_copy.start()

    def back_whole(kind, d, count):
        return pltpu.make_async_remote_copy(
            landed.at[0, 0, pl.ds(0, count)], landed.at[0, 0, pl.ds(0, count)],
            back_send.at[kind, d], back_recv.at[kind, d],
            device_id=partner, device_id_type=MESH,
        )
    for kind in (1, 0):
        for d in range(NEAR + 1):
            back_whole(kind, d, lanes - (d == 0)).wait_recv()
        for i in range(lanes):
            acc = landed[kind, 0, i].astype(F32)
            for d in range(1, NEAR + 1):
                acc = acc + landed[kind, d, i].astype(F32)
            dkv_ref[kind, :, pl.ds(i * DIM, DIM)] = acc.astype(BF16)

    for kind in range(2):
        for d in range(NEAR + 1):
            whole(keys, kind, d, ROWS - (piece if d == 0 else 0)).wait_send()
            back_whole(kind, d, lanes - (d == 0)).wait_send()
        for e in range(NEAR):
            relayed(kind, e).wait_send()
            swap(kind, e).wait_send()
    o_copy.wait()
    dq_copy.wait()


def on_device(blocks, lanes, queries, kv_cache, grad_out, positions):
    piece = kv_cache.shape[1]
    wide = kv_cache.shape[2]
    sem = pltpu.SemaphoreType.DMA
    any_spec = pl.BlockSpec(memory_space=pl.ANY)
    vmem_spec = pl.BlockSpec(memory_space=pltpu.VMEM)
    return pl.pallas_call(
        functools.partial(kernel, blocks, lanes),
        out_shape=(
            jax.ShapeDtypeStruct(queries.shape, BF16),
            jax.ShapeDtypeStruct(queries.shape, BF16),
            jax.ShapeDtypeStruct(kv_cache.shape, BF16),
        ),
        in_specs=[any_spec, any_spec, any_spec, vmem_spec],
        out_specs=(any_spec, any_spec, vmem_spec),
        scratch_shapes=[
            pltpu.VMEM((2, piece, wide), BF16),
            pltpu.VMEM((COLS, DIM), BF16),
            pltpu.VMEM((COLS, DIM), BF16),
            pltpu.VMEM((DIM, COLS), BF16),
            pltpu.VMEM((DIM, COLS), BF16),
            pltpu.VMEM((SLOTS, ROWS, DIM), BF16),
            pltpu.VMEM((SLOTS, ROWS, DIM), BF16),
            pltpu.VMEM((DIM, SLOTS * ROWS), BF16),
            pltpu.VMEM((DIM, SLOTS * ROWS), BF16),
            pltpu.VMEM((SLOTS, ROWS, ROWS), F32),
            pltpu.VMEM((1, COLS), F32),
            pltpu.VMEM((1, COLS), F32),
            pltpu.VMEM((SLOTS, 1, COLS), F32),
            pltpu.VMEM((SLOTS * ROWS, COLS), F32),
            pltpu.VMEM((SLOTS * ROWS, COLS), BF16),
            pltpu.VMEM((SLOTS * ROWS, COLS), F32),
            pltpu.VMEM((SLOTS * ROWS, COLS), BF16),
            pltpu.VMEM((1, COLS), F32),
            pltpu.VMEM((DIM, COLS), BF16),
            pltpu.VMEM((2, NEAR, ROWS, DIM), F32),
            pltpu.VMEM((2, NEAR, ROWS, DIM), F32),
            pltpu.VMEM((2, NEAR + 1, ROWS, DIM), BF16),
            pltpu.VMEM((2, NEAR + 1, lanes, piece, DIM), BF16),
            pltpu.VMEM(queries.shape, BF16),
            pltpu.VMEM(queries.shape, BF16),
            sem((3 + 2 * HEADS,)),
            sem((2,)),
            sem((2, NEAR + 1)),
            sem((2, NEAR + 1)),
            sem((2, NEAR)),
            sem((2, NEAR)),
            sem((2, NEAR + 1)),
            sem((2, NEAR + 1)),
            sem((2, NEAR)),
            sem((2, NEAR)),
        ],
        compiler_params=pltpu.CompilerParams(
            collective_id=0, has_side_effects=True, vmem_limit_bytes=48 * 1024 * 1024
        ),
    )(queries, kv_cache, grad_out, positions.reshape(1, ROWS))


def solution(mesh):
    return jax.shard_map(
        functools.partial(on_device, mesh.shape["ctx"], mesh.shape["tsp"]),
        mesh=mesh,
        in_specs=(
            P(None, "ctx", "tsp"),
            P(None, ("ctx", "tsp"), None),
            P(None, "ctx", "tsp"),
            P("ctx"),
        ),
        out_specs=(P(None, "ctx", "tsp"), P(None, "ctx", "tsp"), P(None, ("ctx", "tsp"), None)),
        check_vma=False,
    )
```

time: 228 us -> 54.9 us (0.24)
  the two profiles are of different devices: /device:TPU:32 before, /device:TPU:1 now
where the time goes in v1:
time: 54.9 us; the launch traced here: 54.7 us
  Pallas kernels  48.6 us (89%)
  local copies, waits for them, and re-layouts  5.42 us (10%)
  between operations  0.65 us (1%)
    pallas_call x1, Pallas kernels, on_device(): pl.pallas_call(functools.partial(kernel, blocks, lanes), out_shape=(jax.S...  48.6 us
    unnamed x11, local copies, waits for them, and re-layouts  5.42 us

profile of v1, /device:TPU:1, one launch (start us, length us, event | category | flops | bytes accessed | tf_op | source)
XLA Modules:
  0.0 54.7 jit_solution(14042863438792989331)
XLA Ops:
  0.6 0.0 copy-start.3
  0.6 0.6 %copy-done.3 = s32[128]{0:T(128)S(1)} copy-done((s32[128]{0:T(128)S(1)}, s32[128]{0:T(128)}, u32[]{:S(2)}) %copy-start.3) | copy-done | bytes 536
  1.3 0.0 copy-start
  1.3 0.9 %copy-done = bf16[2,128,512]{2,1,0:T(8,128)(2,1)S(1)} copy-done((bf16[2,128,512]{2,1,0:T(8,128)(2,1)S(1)}, bf16[2,128,512]{2,1,0:T(8,128)(2,1)}, u32[]{:S(2)}) %copy-start) | copy-done | bytes 262168
  2.2 0.0 copy-start.1
  2.2 0.9 %copy-done.1 = bf16[2,128,512]{2,1,0:T(8,128)(2,1)S(1)} copy-done((bf16[2,128,512]{2,1,0:T(8,128)(2,1)S(1)}, bf16[2,128,512]{2,1,0:T(8,128)(2,1)}, u32[]{:S(2)}) %copy-start.1) | copy-done | bytes 262168
  3.2 0.0 copy-start.2
  3.2 0.8 %copy-done.2 = bf16[2,16,1024]{2,1,0:T(8,128)(2,1)S(1)} copy-done((bf16[2,16,1024]{2,1,0:T(8,128)(2,1)S(1)}, bf16[2,16,1024]{2,1,0:T(8,128)(2,1)}, u32[]{:S(2)}) %copy-start.2) | copy-done | bytes 65560
  4.0 48.6 %shard_map.67 = (bf16[2,128,512]{2,1,0:T(8,128)(2,1)S(1)}, bf16[2,128,512]{2,1,0:T(8,128)(2,1)S(1)}, bf16[2,16,1024]{2,1,0:T(8,128)(2,1)S(1)}) custom-call(bf16[2,128,512]{2,1,0:T(8,128)(2,1)S(1)} %copy-done, bf16[2,16,1024]{2,1,0:T(8,128)(2,1)S(1)} %copy-done.2, bf16[2,128,512]{2,1,0:T(8,128)(2,1)S(1)} %copy-done.1, s32[1,128]{1,0:T(1,128)S(1)} %bitcast.1), custom_call_target="tpu_custom_call" | custom-call | tf_op jit(solution)/shard_map/pallas_call | solution.py:319
  52.6 0.7 %copy.10 = bf16[2,128,512]{2,1,0:T(8,128)(2,1)} copy(bf16[2,128,512]{2,1,0:T(8,128)(2,1)S(1)} %get-tuple-element.6) | data formatting | bytes 524288
  53.3 0.7 %copy.11 = bf16[2,128,512]{2,1,0:T(8,128)(2,1)} copy(bf16[2,128,512]{2,1,0:T(8,128)(2,1)S(1)} %get-tuple-element.7) | data formatting | bytes 524288
  54.0 0.6 %copy.12 = bf16[2,16,1024]{2,1,0:T(8,128)(2,1)} copy(bf16[2,16,1024]{2,1,0:T(8,128)(2,1)S(1)} %get-tuple-element.8) | data formatting | bytes 131072
Async XLA Ops:
  0.6 0.7 %copy-start.3 = (s32[128]{0:T(128)S(1)}, s32[128]{0:T(128)}, u32[]{:S(2)}) copy-start(s32[128]{0:T(128)} %param.7) | copy-start | bytes 1540
  1.3 0.9 %copy-start = (bf16[2,128,512]{2,1,0:T(8,128)(2,1)S(1)}, bf16[2,128,512]{2,1,0:T(8,128)(2,1)}, u32[]{:S(2)}) copy-start(bf16[2,128,512]{2,1,0:T(8,128)(2,1)} %q_hbm.1) | copy-start | bytes 786436
  2.2 0.9 %copy-start.1 = (bf16[2,128,512]{2,1,0:T(8,128)(2,1)S(1)}, bf16[2,128,512]{2,1,0:T(8,128)(2,1)}, u32[]{:S(2)}) copy-start(bf16[2,128,512]{2,1,0:T(8,128)(2,1)} %g_hbm.1) | copy-start | bytes 786436
  3.2 0.8 %copy-start.2 = (bf16[2,16,1024]{2,1,0:T(8,128)(2,1)S(1)}, bf16[2,16,1024]{2,1,0:T(8,128)(2,1)}, u32[]{:S(2)}) copy-start(bf16[2,16,1024]{2,1,0:T(8,128)(2,1)} %kv_hbm.1) | copy-start | bytes 196612

commit v2 on v1

--- a/solution.py
+++ b/solution.py
@@ -16,6 +16,7 @@
 NEAR = SPAN // 2
 SLOTS = SPAN + 1
 HEADS = LAYERS * GROUP
+DIRECT = (2, 4, 1, 0)
 COLS = HEADS * ROWS
 CHUNK = 256
 SCALE = DIM ** (-0.5)
@@ -32,12 +33,12 @@
 
 def kernel(
     blocks, lanes,
-    q_hbm, kv_hbm, g_hbm, pos_ref,
-    o_hbm, dq_hbm, dkv_ref,
-    kv, qs, gs, q_t, g_t, keys, vals, k_t, v_t, bias,
+    q_hbm, kv_hbm, g_hbm, pos_hbm,
+    o_out, dq_out, dkv_ref,
+    kv, pos_ref, qs, gs, q_t, g_t, keys, vals, k_t, v_t, bias,
     top, total, tops, expo, probs, dprobs, dscores, delta, o_acc,
-    pair_out, pair_in, ready, landed, o_out, dq_out,
-    in_sem, out_sem, kv_send, kv_recv, pair_send, pair_recv,
+    mine, pair_out, pair_in, ready, landed,
+    in_sem, kv_send, kv_recv, pair_send, pair_recv,
     back_send, back_recv, swap_send, swap_recv,
 ):
     c = lax.axis_index("ctx")
@@ -49,22 +50,34 @@
     def lane(i):
         return lax.rem(t + i, lanes)
 
+    chip = c // 2
+
     def ahead(d):
         return lax.rem(c + 2 * d, blocks)
 
     def behind(d):
         return lax.rem(c + blocks - 2 * d, blocks)
 
+    def has_ahead(d):
+        return chip + d < blocks // 2
+
+    def has_behind(d):
+        return chip >= d
+
     barrier = pltpu.get_barrier_semaphore()
     pl.semaphore_signal(barrier, inc=1, device_id=partner, device_id_type=MESH)
-    for d in range(NEAR + 1):
+    for d in DIRECT:
         def hello(i, _, d=d):
             pl.semaphore_signal(barrier, inc=1, device_id=(behind(d), lane(i)), device_id_type=MESH)
             return 0
-        lax.fori_loop(1 if d == 0 else 0, lanes, hello, 0)
+        @pl.when(has_behind(d))
+        def _(d=d, hello=hello):
+            lax.fori_loop(1 if d == 0 else 0, lanes, hello, 0)
 
     kv_copy = pltpu.make_async_copy(kv_hbm, kv, in_sem.at[0])
     kv_copy.start()
+    pos_copy = pltpu.make_async_copy(pos_hbm, pos_ref, in_sem.at[3 + 2 * HEADS])
+    pos_copy.start()
     def loads():
         out = []
         for l in range(LAYERS):
@@ -77,14 +90,14 @@
     for copy in loads():
         copy.start()
     kv_copy.wait()
-    pl.semaphore_wait(barrier, (NEAR + 1) * lanes)
+    pl.semaphore_wait(barrier, lanes * (1 + sum(jnp.where(has_ahead(d), 1, 0) for d in DIRECT[:-1])))
 
     def kv_piece(kind, d, i):
         to = lane(i)
         place = (keys if kind == 0 else vals)
         return pltpu.make_async_remote_copy(
             kv.at[kind, :, pl.ds(pl.multiple_of(to * DIM, DIM), DIM)],
-            place.at[2 * d, pl.ds(pl.multiple_of(t * piece, piece), piece)],
+            place.at[d, pl.ds(pl.multiple_of(t * piece, piece), piece)],
             kv_send.at[kind, d],
             kv_recv.at[kind, d],
             device_id=(ahead(d), to),
@@ -99,11 +112,13 @@
         )
     for kind in range(2):
         own_piece(kind).start()
-        for d in range(NEAR + 1):
+        for d in DIRECT:
             def send(i, _, kind=kind, d=d):
                 kv_piece(kind, d, i).start()
                 return 0
-            lax.fori_loop(1 if d == 0 else 0, lanes, send, 0)
+            @pl.when(has_ahead(d))
+            def _(d=d, send=send):
+                lax.fori_loop(1 if d == 0 else 0, lanes, send, 0)
 
     def whole(buf, kind, d, rows=ROWS):
         return pltpu.make_async_remote_copy(
@@ -115,17 +130,27 @@
         place = (keys if kind == 0 else vals)
         e = d - core
         return pltpu.make_async_remote_copy(
-            place.at[2 * d], place.at[2 * e + 1],
+            place.at[d], place.at[NEAR + 1 + e],
             pair_send.at[kind, e], pair_recv.at[kind, e],
             device_id=partner, device_id_type=MESH,
         )
     def relayed(kind, e):
         place = (keys if kind == 0 else vals)
         return pltpu.make_async_remote_copy(
-            place.at[2 * (e + core)], place.at[2 * e + 1],
+            place.at[e + core], place.at[NEAR + 1 + e],
             pair_send.at[kind, e], pair_recv.at[kind, e],
             device_id=partner, device_id_type=MESH,
         )
+
+    for d in range(1, NEAR + 1):
+        @pl.when(jnp.logical_not(has_behind(d)))
+        def _(d=d):
+            keys[d] = jnp.zeros((ROWS, DIM), BF16)
+            vals[d] = jnp.zeros((ROWS, DIM), BF16)
+        @pl.when(jnp.logical_not(has_ahead(d)))
+        def _(d=d):
+            for kind in range(2):
+                landed[kind, d] = jnp.zeros(landed.shape[2:], BF16)
 
     for copy in loads():
         copy.wait()
@@ -133,10 +158,12 @@
         part = pl.ds(n * ROWS, ROWS)
         q_t[:, part] = qs[part].T
         g_t[:, part] = gs[part].T
+    pos_copy.wait()
     pos = pos_ref[...]
     base = lax.broadcasted_iota(jnp.int32, (ROWS, ROWS), 1) - lax.broadcasted_iota(jnp.int32, (ROWS, ROWS), 0)
     def mask(o, _):
-        distance = base + o * ROWS
+        blocks_back = jnp.where(o <= NEAR, 2 * o, 2 * (o - NEAR) - 1)
+        distance = base + blocks_back * ROWS
         visible = (distance >= 0) & (distance <= pos) & (distance < SPAN * ROWS)
         bias[o] = jnp.where(visible, 0.0, -jnp.inf)
         return 0
@@ -172,25 +199,55 @@
             dprobs[rows_of(o), cut] = dot(block, g_t[:, cut])
         v_t[:, rows_of(o)] = block.T
 
-    def gather(kind, use):
-        own_piece(kind).wait()
-        whole((keys if kind == 0 else vals), kind, 0, ROWS - piece).wait_recv()
-        @pl.when(core == 0)
+    def forward(kind):
+        place = (keys if kind == 0 else vals)
+        return pltpu.make_async_remote_copy(
+            place.at[2], place.at[3],
+            kv_send.at[kind, 3], kv_recv.at[kind, 3],
+            device_id=(ahead(1), t), device_id_type=MESH,
+        )
+    def first(kind):
+        @pl.when(has_behind(2))
         def _():
-            relay(kind, 0).start()
-        use(0)
-        def step(d, _):
-            whole((keys if kind == 0 else vals), kind, d).wait_recv()
-            @pl.when(d - core < NEAR)
+            whole((keys if kind == 0 else vals), kind, 2).wait_recv()
+            @pl.when(has_ahead(1))
+            def _():
+                forward(kind).start()
+        relay(kind, 2).start()
+
+    def gather(kind, use, between=None):
+        place = (keys if kind == 0 else vals)
+        def pair(d):
+            e = d - 1 + core
+            @pl.when((e >= 0) & (e < NEAR))
+            def _():
+                relayed(kind, e).wait_recv()
+                use(NEAR + 1 + e)
+        def order(i):
+            return jnp.where(i == 0, 2, jnp.where(i < 3, i - 1, 7 - i))
+        use(2)
+        def step(i, _):
+            d = order(i)
+            @pl.when(d == 0)
+            def _():
+                own_piece(kind).wait()
+                whole(place, kind, 0, ROWS - piece).wait_recv()
+            @pl.when((d > 0) & has_behind(d))
+            def _():
+                whole(place, kind, d).wait_recv()
+            @pl.when((d - core >= 0) & (d - core < NEAR))
             def _():
                 relay(kind, d).start()
-            use(2 * d)
-            relayed(kind, d - 1).wait_recv()
-            use(2 * d - 1)
+            use(d)
+            pair(order(i - 1))
             return 0
         lax.fori_loop(1, NEAR + 1, step, 0)
-
-    gather(0, score)
+        if between is not None:
+            between()
+        pair(3)
+
+    first(0)
+    gather(0, score, lambda: first(1))
 
     def factor(o, cut):
         return tops[o, :, cut]
@@ -224,31 +281,31 @@
             device_id_type=MESH,
         )
     def give_back(kind, left, right):
-        def odd(i, _):
-            e = NEAR - 1 - i
-            pair_out[kind, e] = dot(left[rows_of(2 * e + 1), :], right[...])
+        odd = dot(left[pl.ds((NEAR + 1) * ROWS, NEAR * ROWS), :], right[...])
+        for e in range(NEAR):
+            pair_out[kind, e] = odd[e * ROWS:(e + 1) * ROWS]
             swap(kind, e).start()
-            return 0
-        lax.fori_loop(0, NEAR, odd, 0)
-        def even(i, _):
+        even = dot(left[pl.ds(0, (NEAR + 1) * ROWS), :], right[...])
+        for d in range(NEAR + 1):
+            mine[kind, d] = even[d * ROWS:(d + 1) * ROWS]
+        def step(i, _):
             d = NEAR - i
-            mine = dot(left[rows_of(2 * d), :], right[...])
             e = d - core
             paired = (e >= 0) & (e < NEAR)
             @pl.when(paired)
             def _():
                 swap(kind, e).wait_recv()
-                both = mine + pair_in[kind, e]
+                both = mine[kind, d] + pair_in[kind, e]
                 ready[kind, d] = (both if kind == 1 else both * SCALE).astype(BF16)
             @pl.when(jnp.logical_not(paired))
             def _():
-                ready[kind, d] = (mine if kind == 1 else mine * SCALE).astype(BF16)
+                ready[kind, d] = (mine[kind, d] if kind == 1 else mine[kind, d] * SCALE).astype(BF16)
             def send(i, _):
                 back_piece(kind, d, i).start()
                 return 0
-            lax.fori_loop(jnp.where(d == 0, 1, 0), lanes, send, 0)
+            lax.fori_loop(jnp.where(d == 0, 1, 0), jnp.where(has_behind(d), lanes, 0), send, 0)
             return 0
-        lax.fori_loop(0, NEAR + 1, even, 0)
+        lax.fori_loop(0, NEAR + 1, step, 0)
         landed[kind, 0, t] = ready[kind, 0, pl.ds(pl.multiple_of(t * piece, piece), piece), :]
 
     give_back(1, probs, gs)
@@ -273,16 +330,12 @@
         l, g = n // GROUP, n % GROUP
         part = pl.ds(n * ROWS, ROWS)
         o_out[l, :, pl.ds(g * DIM, DIM)] = o_acc[:, part].T
-    o_copy = pltpu.make_async_copy(o_out, o_hbm, out_sem.at[0])
-    o_copy.start()
     for i, cut in enumerate(chunks()):
         dq = (dot(k_t[...], dscores[:, cut]) * SCALE).astype(BF16)
         for j in range(CHUNK // ROWS):
             n = i * (CHUNK // ROWS) + j
             l, g = n // GROUP, n % GROUP
             dq_out[l, :, pl.ds(g * DIM, DIM)] = dq[:, j * ROWS:(j + 1) * ROWS].T
-    dq_copy = pltpu.make_async_copy(dq_out, dq_hbm, out_sem.at[1])
-    dq_copy.start()
 
     def back_whole(kind, d, count):
         return pltpu.make_async_remote_copy(
@@ -292,7 +345,9 @@
         )
     for kind in (1, 0):
         for d in range(NEAR + 1):
-            back_whole(kind, d, lanes - (d == 0)).wait_recv()
+            @pl.when(has_ahead(d))
+            def _(kind=kind, d=d):
+                back_whole(kind, d, lanes - (d == 0)).wait_recv()
         for i in range(lanes):
             acc = landed[kind, 0, i].astype(F32)
             for d in range(1, NEAR + 1):
@@ -301,32 +356,48 @@
 
     for kind in range(2):
         for d in range(NEAR + 1):
-            whole(keys, kind, d, ROWS - (piece if d == 0 else 0)).wait_send()
-            back_whole(kind, d, lanes - (d == 0)).wait_send()
+            @pl.when(has_ahead(d) if d != 3 else has_ahead(1) & has_behind(2))
+            def _(kind=kind, d=d):
+                whole(keys, kind, d, ROWS - (piece if d == 0 else 0)).wait_send()
+            @pl.when(has_behind(d))
+            def _(kind=kind, d=d):
+                back_whole(kind, d, lanes - (d == 0)).wait_send()
         for e in range(NEAR):
             relayed(kind, e).wait_send()
             swap(kind, e).wait_send()
-    o_copy.wait()
-    dq_copy.wait()
+
+
+def store(*refs):
+    parts, outs, held, sems = refs[:3], refs[3:6], refs[6:9], refs[9]
+    into = [pltpu.make_async_copy(parts[i], held[i], sems.at[i]) for i in range(3)]
+    out = [pltpu.make_async_copy(held[i], outs[i], sems.at[3 + i]) for i in range(3)]
+    for copy in into:
+        copy.start()
+    for i in range(3):
+        into[i].wait()
+        out[i].start()
+    for copy in out:
+        copy.wait()
 
 
 def on_device(blocks, lanes, queries, kv_cache, grad_out, positions):
     piece = kv_cache.shape[1]
     wide = kv_cache.shape[2]
     sem = pltpu.SemaphoreType.DMA
-    any_spec = pl.BlockSpec(memory_space=pl.ANY)
+    hbm_spec = pl.BlockSpec(memory_space=pltpu.HBM)
     vmem_spec = pl.BlockSpec(memory_space=pltpu.VMEM)
-    return pl.pallas_call(
+    parts = pl.pallas_call(
         functools.partial(kernel, blocks, lanes),
         out_shape=(
             jax.ShapeDtypeStruct(queries.shape, BF16),
             jax.ShapeDtypeStruct(queries.shape, BF16),
             jax.ShapeDtypeStruct(kv_cache.shape, BF16),
         ),
-        in_specs=[any_spec, any_spec, any_spec, vmem_spec],
-        out_specs=(any_spec, any_spec, vmem_spec),
+        in_specs=[hbm_spec] * 4,
+        out_specs=(vmem_spec,) * 3,
         scratch_shapes=[
             pltpu.VMEM((2, piece, wide), BF16),
+            pltpu.VMEM((1, ROWS), jnp.int32),
             pltpu.VMEM((COLS, DIM), BF16),
             pltpu.VMEM((COLS, DIM), BF16),
             pltpu.VMEM((DIM, COLS), BF16),
@@ -345,14 +416,12 @@
             pltpu.VMEM((SLOTS * ROWS, COLS), BF16),
             pltpu.VMEM((1, COLS), F32),
             pltpu.VMEM((DIM, COLS), BF16),
+            pltpu.VMEM((2, NEAR + 1, ROWS, DIM), F32),
             pltpu.VMEM((2, NEAR, ROWS, DIM), F32),
             pltpu.VMEM((2, NEAR, ROWS, DIM), F32),
             pltpu.VMEM((2, NEAR + 1, ROWS, DIM), BF16),
             pltpu.VMEM((2, NEAR + 1, lanes, piece, DIM), BF16),
-            pltpu.VMEM(queries.shape, BF16),
-            pltpu.VMEM(queries.shape, BF16),
-            sem((3 + 2 * HEADS,)),
-            sem((2,)),
+            sem((4 + 2 * HEADS,)),
             sem((2, NEAR + 1)),
             sem((2, NEAR + 1)),
             sem((2, NEAR)),
@@ -363,9 +432,17 @@
             sem((2, NEAR)),
         ],
         compiler_params=pltpu.CompilerParams(
-            collective_id=0, has_side_effects=True, vmem_limit_bytes=48 * 1024 * 1024
+            collective_id=0, has_side_effects=True, vmem_limit_bytes=61900 * 1024
         ),
     )(queries, kv_cache, grad_out, positions.reshape(1, ROWS))
+    return pl.pallas_call(
+        store,
+        out_shape=tuple(jax.ShapeDtypeStruct(part.shape, part.dtype) for part in parts),
+        in_specs=[hbm_spec] * 3,
+        out_specs=(hbm_spec,) * 3,
+        scratch_shapes=[pltpu.VMEM(part.shape, part.dtype) for part in parts] + [sem((6,))],
+        compiler_params=pltpu.CompilerParams(vmem_limit_bytes=61900 * 1024),
+    )(*parts)
 
 
 def solution(mesh):

time: 54.9 us -> 48.3 us (0.88)
  the two profiles are of different devices: /device:TPU:1 before, /device:TPU:24 now
where the time goes in v2:
time: 48.3 us; the launch traced here: 48.1 us
  Pallas kernels  47.5 us (98%)
  between operations  0.64 us (1%)
    pallas_call x1, Pallas kernels, on_device(): pl.pallas_call(functools.partial(kernel, blocks, lanes), out_shape=(jax.S...  45.7 us
    pallas_call x1, Pallas kernels, on_device(): pl.pallas_call(store, out_shape=tuple((jax.ShapeDtypeStruct(part.shape, p...  1.8 us

profile of v2, /device:TPU:24, one launch (start us, length us, event | category | flops | bytes accessed | tf_op | source)
XLA Modules:
  0.0 48.1 jit_solution(8327016778112882946)
XLA Ops:
  0.6 45.7 %shard_map.67 = (bf16[2,128,512]{2,1,0:T(8,128)(2,1)}, bf16[2,128,512]{2,1,0:T(8,128)(2,1)}, bf16[2,16,1024]{2,1,0:T(8,128)(2,1)}) custom-call(bf16[2,128,512]{2,1,0:T(8,128)(2,1)} %q_hbm.1, bf16[2,16,1024]{2,1,0:T(8,128)(2,1)} %kv_hbm.1, bf16[2,128,512]{2,1,0:T(8,128)(2,1)} %g_hbm.1, s32[1,128]{1,0:T(1,128)} %bitcast.1), custom_call_target="tpu_custom_call" | custom-call | tf_op jit(solution)/shard_map/pallas_call | solution.py:389
  46.3 1.8 %shard_map.68 = (bf16[2,128,512]{2,1,0:T(8,128)(2,1)}, bf16[2,128,512]{2,1,0:T(8,128)(2,1)}, bf16[2,16,1024]{2,1,0:T(8,128)(2,1)}) custom-call(bf16[2,128,512]{2,1,0:T(8,128)(2,1)} %get-tuple-element.6.refs_0_, bf16[2,128,512]{2,1,0:T(8,128)(2,1)} %get-tuple-element.7.refs_1_, bf16[2,16,1024]{2,1,0:T(8,128)(2,1)} %get-tuple-element.8.refs_2_), custom_call_target="tpu_custom_call" | custom-call | tf_op jit(solution)/shard_map/pallas_call | solution.py:438

commit v3 on v2

--- a/solution.py
+++ b/solution.py
@@ -16,7 +16,7 @@
 NEAR = SPAN // 2
 SLOTS = SPAN + 1
 HEADS = LAYERS * GROUP
-DIRECT = (2, 4, 1, 0)
+DIRECT = (2, 1, 0)
 COLS = HEADS * ROWS
 CHUNK = 256
 SCALE = DIM ** (-0.5)
@@ -87,8 +87,6 @@
                 out.append(pltpu.make_async_copy(q_hbm.at[l, :, cut], qs.at[pl.ds(n * ROWS, ROWS)], in_sem.at[1 + n]))
                 out.append(pltpu.make_async_copy(g_hbm.at[l, :, cut], gs.at[pl.ds(n * ROWS, ROWS)], in_sem.at[1 + HEADS + n]))
         return out
-    for copy in loads():
-        copy.start()
     kv_copy.wait()
     pl.semaphore_wait(barrier, lanes * (1 + sum(jnp.where(has_ahead(d), 1, 0) for d in DIRECT[:-1])))
 
@@ -119,6 +117,9 @@
             @pl.when(has_ahead(d))
             def _(d=d, send=send):
                 lax.fori_loop(1 if d == 0 else 0, lanes, send, 0)
+
+    for copy in loads():
+        copy.start()
 
     def whole(buf, kind, d, rows=ROWS):
         return pltpu.make_async_remote_copy(
@@ -199,20 +200,21 @@
             dprobs[rows_of(o), cut] = dot(block, g_t[:, cut])
         v_t[:, rows_of(o)] = block.T
 
-    def forward(kind):
-        place = (keys if kind == 0 else vals)
-        return pltpu.make_async_remote_copy(
-            place.at[2], place.at[3],
-            kv_send.at[kind, 3], kv_recv.at[kind, 3],
-            device_id=(ahead(1), t), device_id_type=MESH,
+    def forward(kind, hop):
+        place = (keys if kind == 0 else vals)
+        return pltpu.make_async_remote_copy(
+            place.at[2], place.at[2 + hop],
+            kv_send.at[kind, 2 + hop], kv_recv.at[kind, 2 + hop],
+            device_id=(ahead(hop), t), device_id_type=MESH,
         )
     def first(kind):
         @pl.when(has_behind(2))
         def _():
             whole((keys if kind == 0 else vals), kind, 2).wait_recv()
-            @pl.when(has_ahead(1))
-            def _():
-                forward(kind).start()
+            for hop in (2, 1):
+                @pl.when(has_ahead(hop))
+                def _(hop=hop):
+                    forward(kind, hop).start()
         relay(kind, 2).start()
 
     def gather(kind, use, between=None):
@@ -262,7 +264,6 @@
         for cut in chunks():
             probs[rows_of(o), cut] = (expo[rows_of(o), cut] * factor(o, cut)).astype(BF16)
         return 0
-    lax.fori_loop(0, SLOTS, soft, 0)
 
     def swap(kind, e):
         return pltpu.make_async_remote_copy(
@@ -280,11 +281,13 @@
             device_id=(behind(d), to),
             device_id_type=MESH,
         )
-    def give_back(kind, left, right):
+    def give_back(kind, prepare, left, right):
+        lax.fori_loop(NEAR + 1, SLOTS, prepare, 0)
         odd = dot(left[pl.ds((NEAR + 1) * ROWS, NEAR * ROWS), :], right[...])
         for e in range(NEAR):
-            pair_out[kind, e] = odd[e * ROWS:(e + 1) * ROWS]
+            pair_out[kind, e] = odd[e * ROWS:(e + 1) * ROWS].astype(BF16)
             swap(kind, e).start()
+        lax.fori_loop(0, NEAR + 1, prepare, 0)
         even = dot(left[pl.ds(0, (NEAR + 1) * ROWS), :], right[...])
         for d in range(NEAR + 1):
             mine[kind, d] = even[d * ROWS:(d + 1) * ROWS]
@@ -295,7 +298,7 @@
             @pl.when(paired)
             def _():
                 swap(kind, e).wait_recv()
-                both = mine[kind, d] + pair_in[kind, e]
+                both = mine[kind, d] + pair_in[kind, e].astype(F32)
                 ready[kind, d] = (both if kind == 1 else both * SCALE).astype(BF16)
             @pl.when(jnp.logical_not(paired))
             def _():
@@ -308,7 +311,7 @@
         lax.fori_loop(0, NEAR + 1, step, 0)
         landed[kind, 0, t] = ready[kind, 0, pl.ds(pl.multiple_of(t * piece, piece), piece), :]
 
-    give_back(1, probs, gs)
+    give_back(1, soft, probs, gs)
 
     gather(1, value)
 
@@ -322,9 +325,8 @@
             p = expo[rows_of(o), cut] * factor(o, cut)
             dscores[rows_of(o), cut] = (p * (dprobs[rows_of(o), cut] - delta[:, cut])).astype(BF16)
         return 0
-    lax.fori_loop(0, SLOTS, soft_back, 0)
-
-    give_back(0, dscores, qs)
+
+    give_back(0, soft_back, dscores, qs)
 
     for n in range(HEADS):
         l, g = n // GROUP, n % GROUP
@@ -356,7 +358,7 @@
 
     for kind in range(2):
         for d in range(NEAR + 1):
-            @pl.when(has_ahead(d) if d != 3 else has_ahead(1) & has_behind(2))
+            @pl.when(has_ahead(d) if d < 3 else has_ahead(d - 2) & has_behind(2))
             def _(kind=kind, d=d):
                 whole(keys, kind, d, ROWS - (piece if d == 0 else 0)).wait_send()
             @pl.when(has_behind(d))
@@ -417,8 +419,8 @@
             pltpu.VMEM((1, COLS), F32),
             pltpu.VMEM((DIM, COLS), BF16),
             pltpu.VMEM((2, NEAR + 1, ROWS, DIM), F32),
-            pltpu.VMEM((2, NEAR, ROWS, DIM), F32),
-            pltpu.VMEM((2, NEAR, ROWS, DIM), F32),
+            pltpu.VMEM((2, NEAR, ROWS, DIM), BF16),
+            pltpu.VMEM((2, NEAR, ROWS, DIM), BF16),
             pltpu.VMEM((2, NEAR + 1, ROWS, DIM), BF16),
             pltpu.VMEM((2, NEAR + 1, lanes, piece, DIM), BF16),
             sem((4 + 2 * HEADS,)),

time: 48.3 us -> 47.1 us (0.975)
  the two profiles are of different devices: /device:TPU:24 before, /device:TPU:40 now
where the time goes in v3:
time: 47.1 us; the launch traced here: 46.8 us
  Pallas kernels  46.2 us (98%)
  between operations  0.64 us (1%)
    pallas_call x1, Pallas kernels, on_device(): pl.pallas_call(functools.partial(kernel, blocks, lanes), out_shape=(jax.S...  44.4 us
    pallas_call x1, Pallas kernels, on_device(): pl.pallas_call(store, out_shape=tuple((jax.ShapeDtypeStruct(part.shape, p...  1.8 us

profile of v3, /device:TPU:40, one launch (start us, length us, event | category | flops | bytes accessed | tf_op | source)
XLA Modules:
  0.0 46.8 jit_solution(5946634781161614136)
XLA Ops:
  0.6 44.4 %shard_map.67 = (bf16[2,128,512]{2,1,0:T(8,128)(2,1)}, bf16[2,128,512]{2,1,0:T(8,128)(2,1)}, bf16[2,16,1024]{2,1,0:T(8,128)(2,1)}) custom-call(bf16[2,128,512]{2,1,0:T(8,128)(2,1)} %q_hbm.1, bf16[2,16,1024]{2,1,0:T(8,128)(2,1)} %kv_hbm.1, bf16[2,128,512]{2,1,0:T(8,128)(2,1)} %g_hbm.1, s32[1,128]{1,0:T(1,128)} %bitcast.1), custom_call_target="tpu_custom_call" | custom-call | tf_op jit(solution)/shard_map/pallas_call | solution.py:391
  45.0 1.8 %shard_map.68 = (bf16[2,128,512]{2,1,0:T(8,128)(2,1)}, bf16[2,128,512]{2,1,0:T(8,128)(2,1)}, bf16[2,16,1024]{2,1,0:T(8,128)(2,1)}) custom-call(bf16[2,128,512]{2,1,0:T(8,128)(2,1)} %get-tuple-element.6.refs_0_, bf16[2,128,512]{2,1,0:T(8,128)(2,1)} %get-tuple-element.7.refs_1_, bf16[2,16,1024]{2,1,0:T(8,128)(2,1)} %get-tuple-element.8.refs_2_), custom_call_target="tpu_custom_call" | custom-call | tf_op jit(solution)/shard_map/pallas_call | solution.py:440

commit v4 on v3

--- a/solution.py
+++ b/solution.py
@@ -34,11 +34,11 @@
 def kernel(
     blocks, lanes,
     q_hbm, kv_hbm, g_hbm, pos_hbm,
-    o_out, dq_out, dkv_ref,
+    o_hbm, dq_hbm, dkv_ref,
     kv, pos_ref, qs, gs, q_t, g_t, keys, vals, k_t, v_t, bias,
     top, total, tops, expo, probs, dprobs, dscores, delta, o_acc,
-    mine, pair_out, pair_in, ready, landed,
-    in_sem, kv_send, kv_recv, pair_send, pair_recv,
+    mine, pair_out, pair_in, ready, landed, o_out, dq_out,
+    in_sem, out_sem, kv_send, kv_recv, pair_send, pair_recv,
     back_send, back_recv, swap_send, swap_recv,
 ):
     c = lax.axis_index("ctx")
@@ -332,6 +332,8 @@
         l, g = n // GROUP, n % GROUP
         part = pl.ds(n * ROWS, ROWS)
         o_out[l, :, pl.ds(g * DIM, DIM)] = o_acc[:, part].T
+    o_copy = pltpu.make_async_copy(o_out, o_hbm, out_sem.at[0])
+    o_copy.start()
     for i, cut in enumerate(chunks()):
         dq = (dot(k_t[...], dscores[:, cut]) * SCALE).astype(BF16)
         for j in range(CHUNK // ROWS):
@@ -339,6 +341,9 @@
             l, g = n // GROUP, n % GROUP
             dq_out[l, :, pl.ds(g * DIM, DIM)] = dq[:, j * ROWS:(j + 1) * ROWS].T
 
+    dq_copy = pltpu.make_async_copy(dq_out, dq_hbm, out_sem.at[1])
+    dq_copy.start()
+
     def back_whole(kind, d, count):
         return pltpu.make_async_remote_copy(
             landed.at[0, 0, pl.ds(0, count)], landed.at[0, 0, pl.ds(0, count)],
@@ -346,6 +351,9 @@
             device_id=partner, device_id_type=MESH,
         )
     for kind in (1, 0):
+        if kind == 0:
+            o_copy.wait()
+            dq_copy.wait()
         for d in range(NEAR + 1):
             @pl.when(has_ahead(d))
             def _(kind=kind, d=d):
@@ -396,7 +404,7 @@
             jax.ShapeDtypeStruct(kv_cache.shape, BF16),
         ),
         in_specs=[hbm_spec] * 4,
-        out_specs=(vmem_spec,) * 3,
+        out_specs=(hbm_spec, hbm_spec, vmem_spec),
         scratch_shapes=[
             pltpu.VMEM((2, piece, wide), BF16),
             pltpu.VMEM((1, ROWS), jnp.int32),
@@ -423,7 +431,10 @@
             pltpu.VMEM((2, NEAR, ROWS, DIM), BF16),
             pltpu.VMEM((2, NEAR + 1, ROWS, DIM), BF16),
             pltpu.VMEM((2, NEAR + 1, lanes, piece, DIM), BF16),
+            pltpu.VMEM(queries.shape, BF16),
+            pltpu.VMEM(queries.shape, BF16),
             sem((4 + 2 * HEADS,)),
+            sem((2,)),
             sem((2, NEAR + 1)),
             sem((2, NEAR + 1)),
             sem((2, NEAR)),

time: 47.1 us -> 46.9 us (level)
  no operation moved by 1% of the time
where the time goes in v4:
time: 46.9 us; the launch traced here: 46.6 us
  Pallas kernels  46 us (98%)
  between operations  0.64 us (1%)
    pallas_call x1, Pallas kernels, on_device(): pl.pallas_call(functools.partial(kernel, blocks, lanes), out_shape=(jax.S...  44.2 us
    pallas_call x1, Pallas kernels, on_device(): pl.pallas_call(store, out_shape=tuple((jax.ShapeDtypeStruct(part.shape, p...  1.8 us

profile of v4, /device:TPU:40, one launch (start us, length us, event | category | flops | bytes accessed | tf_op | source)
XLA Modules:
  0.0 46.6 jit_solution(2990072650754252278)
XLA Ops:
  0.6 44.2 %shard_map.67 = (bf16[2,128,512]{2,1,0:T(8,128)(2,1)}, bf16[2,128,512]{2,1,0:T(8,128)(2,1)}, bf16[2,16,1024]{2,1,0:T(8,128)(2,1)}) custom-call(bf16[2,128,512]{2,1,0:T(8,128)(2,1)} %q_hbm.1, bf16[2,16,1024]{2,1,0:T(8,128)(2,1)} %kv_hbm.1, bf16[2,128,512]{2,1,0:T(8,128)(2,1)} %g_hbm.1, s32[1,128]{1,0:T(1,128)} %bitcast.1), custom_call_target="tpu_custom_call" | custom-call | tf_op jit(solution)/shard_map/pallas_call | solution.py:399
  44.8 1.8 %shard_map.68 = (bf16[2,128,512]{2,1,0:T(8,128)(2,1)}, bf16[2,128,512]{2,1,0:T(8,128)(2,1)}, bf16[2,16,1024]{2,1,0:T(8,128)(2,1)}) custom-call(bf16[2,128,512]{2,1,0:T(8,128)(2,1)} %get-tuple-element.6.refs_0_, bf16[2,128,512]{2,1,0:T(8,128)(2,1)} %get-tuple-element.7.refs_1_, bf16[2,16,1024]{2,1,0:T(8,128)(2,1)} %get-tuple-element.8.refs_2_), custom_call_target="tpu_custom_call" | custom-call | tf_op jit(solution)/shard_map/pallas_call | solution.py:451
